TPU v7x, 32 devices: a whole 2x2x4 slice. The times are simulated.
32 devices in a mesh: leaf: 8 (over z, y), edge: 4 (over x, core).
Axes of the slice: x: 2, y: 2, z: 4, core: 2. Of those that a mesh axis runs over, the one named last changes fastest.
Arguments:
- positions: float32 [3, 139264], P(None, ('leaf', 'edge')), may hold values from -6 to 6
- density: bfloat16 [3, 139264], P(None, ('leaf', 'edge')), may hold values from -6 to 6
- self_operator: bfloat16 [1632, 1632], P('edge'), may hold values from -0.15625 to 0.15625
- owner: int32 [139264, 1], P(('leaf', 'edge')), may hold values from 0 to 7; in each aligned block of 4352 rows (0 to 4351, 4352 to 8703, ...) at most 816 rows name the same one
- near_tiles: int32 [1632, 3], P(('leaf', 'edge')), may hold values from 0 to 152, as said below
Outputs:
- velocity: float32 [3, 139264], P(None, ('leaf', 'edge'))
Inputs may be any that keep to these rules, and one draw needn't show every extreme that they name: Among the rows of one device, at most 816 name the same owner; some owner reaches 816 in every draw. `near_tiles`: rows list leaves in the order of the points' blocks, 51 rows a leaf. Indices count the lower layer's 51 tiles, then the leaf's own, then the upper layer's. Column 0 names a tile of the lower layer, column 1 one of the upper layer, column 2 any tile.
All inputs are finite; a program needn't handle non-finite values.
Results may differ from a plain program's by a relative error of at most 0.00035.
Values may be sent and summed in bfloat16 or wider, within the bound.
A program may use at most 64 MiB of HBM per device.

v0:
```python
import functools
import math

import jax
import jax.numpy as jnp
from jax import lax
from jax.experimental import pallas as pl
from jax.experimental.pallas import tpu as pltpu
from jax.sharding import PartitionSpec as P

NPT = 544
LANES = 128
GROUPS = 4

reg_square = 0.05
kernel_scale = 1.0 / (8.0 * math.pi)
NT = (((1,), (1,)), ((), ()))
TN = (((0,), (0,)), ((), ()))


def split3(x):
    hi = x.astype(jnp.bfloat16).astype(jnp.float32)
    rest = x - hi
    mid = rest.astype(jnp.bfloat16).astype(jnp.float32)
    return hi, mid, rest - mid


def split2(x):
    hi = x.astype(jnp.bfloat16)
    return hi, (x - hi.astype(jnp.float32)).astype(jnp.bfloat16)


def onehots(leafs, offset, own_ref, row_ref, lane_ref):
    points = own_ref.shape[1]
    win = row_ref.shape[0] // leafs
    chunks = points // LANES
    own = own_ref[...]
    ids = lax.broadcasted_iota(jnp.int32, (leafs, LANES), 0)
    hot = [jnp.where(own[:, c * LANES : (c + 1) * LANES] == ids, 1.0, 0.0) for c in range(chunks)]
    stacked = jnp.concatenate(hot, axis=0).astype(jnp.bfloat16)
    before = lax.broadcasted_iota(jnp.int32, (LANES, 2 * LANES), 0)
    after = lax.broadcasted_iota(jnp.int32, (LANES, 2 * LANES), 1)
    prefix = jnp.where((before < after), 1.0, 0.0).astype(jnp.bfloat16)
    counts = jnp.dot(stacked, prefix, preferred_element_type=jnp.float32)
    carry = jnp.zeros((leafs, LANES), jnp.float32) + offset.astype(jnp.float32)
    row_ids = lax.broadcasted_iota(jnp.int32, (leafs * win, LANES), 0)
    lane_ids = lax.broadcasted_iota(jnp.int32, (LANES, LANES), 0)
    for c in range(chunks):
        block = slice(c * leafs, (c + 1) * leafs)
        here = slice(c * LANES, (c + 1) * LANES)
        place = hot[c] * (counts[block, :LANES] + carry)
        carry = carry + counts[block, LANES:]
        slot = jnp.sum(place, axis=0, keepdims=True).astype(jnp.int32)
        row = own[:, here] * win + (slot >> 7)
        row_ref[:, here] = jnp.where(row == row_ids, 1.0, 0.0).astype(jnp.bfloat16)
        lane_ref[:, here] = jnp.where((slot & 127) == lane_ids, 1.0, 0.0).astype(jnp.bfloat16)


def scatter(leafs, pos_ref, den_ref, row_ref, lane_ref, spread_ref, send_ref):
    rows = row_ref.shape[0]
    win = rows // leafs
    pos = pos_ref[...]
    den = den_ref[...].astype(jnp.float32)
    parts = split3(pos)
    for k in range(12):
        part = den if k >= 9 else parts[k % 3]
        comp = k - 9 if k >= 9 else k // 3
        line = jnp.broadcast_to(part[comp : comp + 1], (16, pos.shape[1])).astype(jnp.bfloat16)
        for r in range(0, rows, 16):
            spread_ref[k * rows + r : k * rows + r + 16, :] = row_ref[r : r + 16, :] * line
    for comp in range(6):
        first, count = (comp * 3, 3) if comp < 3 else (6 + comp, 1)
        placed = lax.dot_general(
            spread_ref[first * rows : (first + count) * rows, :], lane_ref[...], NT,
            preferred_element_type=jnp.float32,
        )
        total = placed[:rows]
        for part in range(1, count):
            total = total + placed[part * rows : (part + 1) * rows]
        for o in range(leafs):
            send_ref[o, comp] = total[o * win : (o + 1) * win]


def assemble(starts, recv_ref, tiles_ref):
    tiles_ref[...] = jnp.zeros_like(tiles_ref)
    win = recv_ref.shape[2]
    for l, start in enumerate(starts):
        for comp in range(6):
            tiles_ref[start : start + win, comp, :] += recv_ref[l, comp]


def features(tile, weight_ref, value_ref, target_ref):
    row = lax.broadcasted_iota(jnp.int32, (8, LANES), 0)
    first, last = row < 3, row == 7
    one = jnp.where(row == 6, 1.0, 0.0)
    pos = jnp.where(first, tile, 0.0)
    force = jnp.where(first, pltpu.roll(tile, 5, 0), 0.0)
    twice = force + jnp.where(first, 0.0, tile)
    hi, mid, low = split3(pos)
    hi_next, mid_next, low_next = (pltpu.roll(part, 3, 0) for part in (hi, mid, low))
    square = jnp.sum(pos * pos, axis=0, keepdims=True)
    along = jnp.sum(pos * force, axis=0, keepdims=True)
    zero = jnp.zeros_like(pos)
    pairs = (hi + hi_next, hi + mid_next, mid + low_next)
    r2_rows = [jnp.where(last, q, one - 2.0 * pair) for q, pair in zip(split3(square), pairs)]
    df_rows = [jnp.where(last, q, f) for q, f in zip(split3(-along), (twice, force, zero))]
    weight_ref[...] = jnp.concatenate(
        [jnp.concatenate(r2_rows + [zero], axis=0), jnp.concatenate(df_rows + [zero], axis=0)], axis=1
    ).astype(jnp.bfloat16)
    if target_ref is not None:
        pairs = (hi + mid_next, low + hi_next, mid + hi_next)
        fixed = jnp.where(last, 1.0, 0.0)
        rows = [fixed + pair + one * q for q, pair in zip(split3(square + reg_square), pairs)]
        target_ref[...] = jnp.concatenate(rows + [zero], axis=0).astype(jnp.bfloat16)
    a_low = one - hi
    value = jnp.concatenate([force, force, a_low - mid_next, a_low], axis=1)
    value_ref[...] = jnp.concatenate([value, jnp.zeros_like(value)], axis=0).astype(jnp.bfloat16)


def near_tile(tile, target, sources):
    blocks, values = [], []
    for weight, value in sources:
        both = lax.dot_general(weight, target, TN, preferred_element_type=jnp.float32)
        inverse = lax.rsqrt(both[:LANES])
        along = both[LANES:] * inverse * (inverse * inverse)
        blocks.extend(split2(inverse) + split2(along))
        values.append(value)
    sums = jnp.dot(
        jnp.concatenate(values, axis=1), jnp.concatenate(blocks, axis=0),
        preferred_element_type=jnp.float32,
    )[:8]
    row = lax.broadcasted_iota(jnp.int32, (8, LANES), 0)
    pos = jnp.where(row < 3, tile, 0.0)
    return (sums + pltpu.roll(sums, 5, 0) + pos * sums[6:7]) * kernel_scale


def gather(leafs, get_near, row_ref, lane_ref, self_ref, out_ref):
    rows = row_ref.shape[0]
    points = out_ref.shape[1]
    split = []
    for comp in range(3):
        block = jnp.concatenate([get_near(o, comp) for o in range(leafs)], axis=0)
        split.append(jnp.concatenate([p.astype(jnp.bfloat16) for p in split3(block)], axis=1))
    near = jnp.concatenate(split, axis=0)
    for begin in range(0, points, 2 * LANES):
        here = slice(begin, begin + 2 * LANES)
        lane = lane_ref[:, here]
        found = jnp.dot(
            near, jnp.concatenate([lane, lane, lane], axis=0), preferred_element_type=jnp.float32
        )
        row = row_ref[:, here].astype(jnp.float32)
        for comp in range(3):
            picked = found[comp * rows : (comp + 1) * rows] * row
            out_ref[comp : comp + 1, here] = (
                jnp.sum(picked, axis=0, keepdims=True) + self_ref[comp : comp + 1, here]
            )


def pre_kernel(leafs, slots, own_ref, pos_ref, den_ref, send_ref, row_ref, lane_ref, spread_ref):
    offset = lax.rem(lax.axis_index("leaf") * slots, LANES)
    onehots(leafs, offset, own_ref, row_ref, lane_ref)
    scatter(leafs, pos_ref, den_ref, row_ref, lane_ref, spread_ref, send_ref)


def build_layer(tiles, starts, layer, recv, tiles_ref, weight_ref, value_ref, target_ref):
    assemble(starts, recv, tiles_ref.at[layer])

    def build(j, carry):
        index = layer * tiles + j
        features(tiles_ref[layer, j], weight_ref.at[index], value_ref.at[index],
                 target_ref.at[j] if layer == 1 else None)
        return carry

    lax.fori_loop(0, tiles, build, 0, unroll=3)


def near_steps(begin, end, tiles, lists_ref, tiles_ref, weight_ref, value_ref, target_ref, near_ref, unroll):
    def step(j, carry):
        indices = [tiles + j] + [lists_ref[column, j] for column in range(3)]
        near_ref[j] = near_tile(tiles_ref[1, j], target_ref[j],
                                [(weight_ref[i], value_ref[i]) for i in indices])
        return carry

    lax.fori_loop(begin, end, step, 0, unroll=unroll)


def near_kernel(tiles, starts, lists_ref, own_ref, low_ref, high_ref, ret_ref, tiles_ref, *matrices):
    *features_refs, near_ref = matrices
    for layer, recv in enumerate((low_ref, own_ref, high_ref)):
        build_layer(tiles, starts, layer, recv, tiles_ref, *features_refs)
    near_ref[...] = jnp.zeros_like(near_ref)
    near_steps(0, tiles, tiles, lists_ref, tiles_ref, *matrices, 3)
    for l, start in enumerate(starts):
        for comp in range(3):
            ret_ref[l, comp] = near_ref[start : start + ret_ref.shape[2], comp, :]


def post_kernel(leafs, back_ref, row_ref, lane_ref, self_ref, out_ref):
    gather(leafs, lambda o, comp: back_ref[o, comp], row_ref, lane_ref, self_ref, out_ref)


def fused_kernel(leafs, edges, slots, tiles, starts, lists_hbm, own_hbm, pos_hbm, den_ref, operator_ref,
                 out_ref, lists_ref, own_ref, pos_ref, cells_ref, wide_ref, row_ref, lane_ref, spread_ref, send_ref, windows_ref,
                 tiles_ref, weight_ref, value_ref, target_ref, near_ref, ret_ref, back_ref,
                 group_ref, partial_ref, parts_ref, whole_ref, self_ref,
                 load_sems, cell_sems, part_sems, point_sems, edge_sems, back_sems):
    loads = [pltpu.make_async_copy(own_hbm, own_ref, load_sems.at[0]),
             pltpu.make_async_copy(pos_hbm, pos_ref, load_sems.at[1]),
             pltpu.make_async_copy(lists_hbm, lists_ref, load_sems.at[2])]
    for load in loads:
        load.start()
    leaf, edge = lax.axis_index("leaf"), lax.axis_index("edge")
    barrier = pltpu.get_barrier_semaphore()
    for d in range(1, leafs):
        pl.semaphore_signal(barrier, inc=1, device_id={"leaf": lax.rem(leaf + d, leafs)})
    for d in range(1, edges):
        pl.semaphore_signal(barrier, inc=1, device_id={"edge": lax.rem(edge + d, edges)})

    def remote(src, dst, sems, index, **device):
        return pltpu.make_async_remote_copy(
            src_ref=src, dst_ref=dst, send_sem=sems.at[0, index], recv_sem=sems.at[1, index],
            device_id=device,
        )

    loads[0].wait()
    onehots(leafs, lax.rem(leaf * slots, LANES), own_ref, row_ref, lane_ref)
    loads[1].wait()
    loads[2].wait()
    scatter(leafs, pos_ref, den_ref, row_ref, lane_ref, spread_ref, send_ref)
    pl.semaphore_wait(barrier, leafs + edges - 2)

    points = []
    for d in range(1, leafs):
        to = lax.rem(leaf + d, leafs)
        points.append(remote(send_ref.at[to], windows_ref.at[1, leaf], point_sems, d, leaf=to))
        points[-1].start()
    count = parts_ref.shape[1]
    wide_ref[...] = jnp.zeros_like(wide_ref)
    dense = den_ref[...].astype(jnp.float32)
    for c in range(count):
        for k in range(3):
            wide_ref[c : c + 1, k * NPT : (k + 1) * NPT] = dense[k : k + 1, c * NPT : (c + 1) * NPT]
    cells_ref[...] = wide_ref[...].astype(jnp.bfloat16)
    cells = []
    for d in range(1, edges):
        to = lax.rem(edge + d, edges)
        cells.append(remote(cells_ref, group_ref.at[edge], cell_sems, d, edge=to))
        cells[-1].start()
    windows_ref[1, leaf] = send_ref[leaf]
    group_ref[edge] = cells_ref[...]

    has_up, has_down = edge < edges - 1, edge > 0

    def forward(source, d):
        up = remote(windows_ref.at[1, source], windows_ref.at[0, source], edge_sems.at[0], d,
                    edge=jnp.minimum(edge + 1, edges - 1))
        down = remote(windows_ref.at[1, source], windows_ref.at[2, source], edge_sems.at[1], d,
                      edge=jnp.maximum(edge - 1, 0))
        return up, down

    def start_forward(source, d):
        up, down = forward(source, d)
        pl.when(has_up)(up.start)
        pl.when(has_down)(down.start)

    start_forward(leaf, 0)
    for copy in cells:
        copy.wait()
    group = group_ref[...].reshape(edges * group_ref.shape[1], group_ref.shape[2])
    partial = lax.dot_general(group, operator_ref[...], NT, preferred_element_type=jnp.float32)
    partial_ref[...] = partial.reshape(partial_ref.shape)
    parts = []
    for d in range(1, edges):
        to = lax.rem(edge + d, edges)
        parts.append(remote(partial_ref.at[to, pl.ds(0, count)], parts_ref.at[edge], part_sems, d, edge=to))
        parts[-1].start()
    parts_ref[edge] = partial_ref[edge, pl.ds(0, count)]

    for d in range(1, leafs):
        points[d - 1].wait()
        start_forward(lax.rem(leaf + leafs - d, leafs), d)

    @pl.when(edge == 0)
    def _():
        windows_ref[0] = jnp.zeros_like(windows_ref[0])

    @pl.when(edge == edges - 1)
    def _():
        windows_ref[2] = jnp.zeros_like(windows_ref[2])

    matrices = (weight_ref, value_ref, target_ref)
    build_layer(tiles, starts, 1, windows_ref.at[1], tiles_ref, *matrices)
    near_ref[...] = jnp.zeros_like(near_ref)
    flights = [forward(lax.rem(leaf + leafs - d, leafs), d) for d in range(leafs)]
    for up, down in flights:
        pl.when(has_down)(up.wait_recv)
    build_layer(tiles, starts, 0, windows_ref.at[0], tiles_ref, *matrices)
    for up, down in flights:
        pl.when(has_up)(down.wait_recv)
        pl.when(has_up)(up.wait_send)
        pl.when(has_down)(down.wait_send)
    build_layer(tiles, starts, 2, windows_ref.at[2], tiles_ref, *matrices)

    win = ret_ref.shape[2]

    unroll = 17 if tiles % 17 == 0 else 1
    middle = tiles * 2 // 3 // unroll * unroll
    first = middle * LANES // slots
    for begin, end, sources in ((0, middle, range(first)), (middle, tiles, range(first, leafs))):
        near_steps(begin, end, tiles, lists_ref, tiles_ref, *matrices, near_ref, unroll)
        for s in sources:
            for comp in range(3):
                ret_ref[s, comp] = near_ref[starts[s] : starts[s] + win, comp, :]

            @pl.when(leaf != s)
            def _(s=s):
                give = pltpu.make_async_remote_copy(
                    src_ref=ret_ref.at[s], dst_ref=back_ref.at[leaf], send_sem=back_sems.at[0, s],
                    recv_sem=back_sems.at[1, leaf], device_id={"leaf": s})
                give.start()

    back_ref[leaf] = ret_ref[leaf]
    for copy in parts:
        copy.wait()
    share = parts_ref.shape[2]
    for e in range(edges):
        whole_ref[:, e * share : (e + 1) * share] = parts_ref[e]
    for c in range(count):
        for k in range(3):
            self_ref[k : k + 1, c * NPT : (c + 1) * NPT] = whole_ref[c : c + 1, k * NPT : (k + 1) * NPT]
    for s in range(leafs):
        @pl.when(leaf != s)
        def _(s=s):
            take = pltpu.make_async_remote_copy(
                src_ref=ret_ref.at[s], dst_ref=back_ref.at[s], send_sem=back_sems.at[0, s],
                recv_sem=back_sems.at[1, s], device_id={"leaf": s})
            take.wait()
    gather(leafs, lambda o, comp: back_ref[o, comp], row_ref, lane_ref, self_ref, out_ref)


VM = pl.BlockSpec(memory_space=pltpu.VMEM)
PARAMS = pltpu.CompilerParams(vmem_limit_bytes=48 * 2**20)


def self_part(density):
    cell_count = density.shape[1] // NPT
    return density.reshape(3, cell_count, NPT).transpose(1, 0, 2).reshape(cell_count, 3 * NPT)


def fast(positions, density, self_operator, owner, near_tiles):
    points = density.shape[1]
    cell_count = points // NPT
    leafs = lax.axis_size("leaf")
    slots = 3 * points // (2 * leafs)
    tiles = slots * leafs // LANES
    starts = [l * slots // LANES for l in range(leafs)]
    win = max((l * slots % LANES + slots - 1) // LANES + 1 for l in range(leafs))
    padded_tiles = -(-max(tiles, starts[-1] + win) // 8) * 8
    rows = leafs * win
    f32, bf16 = jnp.float32, jnp.bfloat16
    shape = jax.ShapeDtypeStruct

    edges = lax.axis_size("edge")
    matrices = [
        pltpu.VMEM((3, padded_tiles, 8, LANES), f32),
        pltpu.VMEM((3 * tiles, 8 * GROUPS, 2 * LANES), bf16),
        pltpu.VMEM((3 * tiles, 16, 4 * LANES), bf16),
        pltpu.VMEM((tiles, 8 * GROUPS, LANES), bf16),
        pltpu.VMEM((padded_tiles, 8, LANES), f32),
    ]
    if leafs <= 8:
        group = -(-cell_count // 16) * 16
        sems = pltpu.SemaphoreType.DMA
        return pl.pallas_call(
            functools.partial(fused_kernel, leafs, edges, slots, tiles, starts),
            out_shape=shape((3, points), f32),
            in_specs=[pl.BlockSpec(memory_space=pltpu.HBM)] * 3 + [VM] * 2,
            out_specs=VM,
            scratch_shapes=[
                pltpu.SMEM((3, tiles), jnp.int32),
                pltpu.VMEM((1, points), jnp.int32),
                pltpu.VMEM((3, points), f32),
                pltpu.VMEM((group, 3 * NPT), bf16),
                pltpu.VMEM((group, 3 * NPT), f32),
                pltpu.VMEM((rows, points), bf16),
                pltpu.VMEM((LANES, points), bf16),
                pltpu.VMEM((12 * rows, points), bf16),
                pltpu.VMEM((leafs, 6, win, LANES), f32),
                pltpu.VMEM((3, leafs, 6, win, LANES), f32),
                *matrices,
                pltpu.VMEM((leafs, 3, win, LANES), f32),
                pltpu.VMEM((leafs, 3, win, LANES), f32),
                pltpu.VMEM((edges, group, 3 * NPT), bf16),
                pltpu.VMEM((edges, group, self_operator.shape[0]), f32),
                pltpu.VMEM((edges, cell_count, self_operator.shape[0]), f32),
                pltpu.VMEM((cell_count, 3 * NPT), f32),
                pltpu.VMEM((3, points), f32),
                sems((3,)), sems((2, edges)), sems((2, edges)), sems((2, leafs)), sems((2, 2, leafs)),
                sems((2, leafs)),
            ],
            compiler_params=pltpu.CompilerParams(
                vmem_limit_bytes=62 * 2**20, collective_id=0, has_side_effects=True
            ),
            name="fused",
        )(near_tiles.T, owner.reshape(1, points), positions, density, self_operator)

    send, row_hot, lane_hot = pl.pallas_call(
        functools.partial(pre_kernel, leafs, slots),
        out_shape=(shape((leafs, 6, win, LANES), f32), shape((rows, points), bf16),
                   shape((LANES, points), bf16)),
        in_specs=[VM] * 3, out_specs=(VM,) * 3,
        scratch_shapes=[pltpu.VMEM((12 * rows, points), bf16)],
        compiler_params=PARAMS, name="pre",
    )(owner.reshape(1, points), positions, density)
    received = lax.all_to_all(send, "leaf", split_axis=0, concat_axis=0, tiled=True)
    up = [(i, i + 1) for i in range(edges - 1)]
    low = lax.ppermute(received, "edge", up)
    high = lax.ppermute(received, "edge", [(b, a) for a, b in up])

    group_rows = lax.all_gather(self_part(density), "edge", axis=0, tiled=True)
    partial_rows = lax.dot_general(group_rows, self_operator, NT, preferred_element_type=f32)
    rows_back = lax.all_to_all(partial_rows, "edge", split_axis=0, concat_axis=1, tiled=True)
    self_velocity = rows_back.reshape(cell_count, 3, NPT).transpose(1, 0, 2).reshape(3, points)

    result = pl.pallas_call(
        functools.partial(near_kernel, tiles, starts),
        out_shape=shape((leafs, 3, win, LANES), f32),
        in_specs=[pl.BlockSpec(memory_space=pltpu.SMEM), VM, VM, VM], out_specs=VM,
        scratch_shapes=matrices,
        compiler_params=PARAMS, name="near",
    )(near_tiles.T, received, low, high)
    back = lax.all_to_all(result, "leaf", split_axis=0, concat_axis=0, tiled=True)
    return pl.pallas_call(
        functools.partial(post_kernel, leafs),
        out_shape=shape((3, points), f32),
        in_specs=[VM] * 4, out_specs=VM, compiler_params=PARAMS, name="post",
    )(back, row_hot, lane_hot, self_velocity)


def solution(mesh):
    placed = (
        P(None, ("leaf", "edge")),
        P(None, ("leaf", "edge")),
        P("edge", None),
        P(("leaf", "edge"), None),
        P(("leaf", "edge"), None),
    )
    return jax.shard_map(
        fast, mesh=mesh, in_specs=placed, out_specs=P(None, ("leaf", "edge")), check_vma=False
    )
```

profile of v0, /device:TPU:1, one launch (start us, length us, event | category | flops | bytes accessed | tf_op | source)
XLA Modules:
  0.0 35.6 jit_solution(12810176263709946798)
XLA Ops:
  0.0 34.1 %fused.1 = f32[3,4352]{1,0:T(4,128)} custom-call(s32[3,51]{1,0:T(4,128)} %bitcast.3, s32[1,4352]{1,0:T(1,128)} %bitcast.2, f32[3,4352]{1,0:T(4,128)} %pos_hbm.1, bf16[3,4352]{1,0:T(4,128)(2,1)} %den_ref.1, bf16[408,1632]{1,0:T(8,128)(2,1)} %operator_ref.1), custom_call_target="tpu_custom_call" | custom-call | tf_op jit(solution)/shard_map/fused/pallas_call | solution.py:374
  34.1 1.5 %copy.7 = f32[3,4352]{1,0:T(4,128)} copy(f32[3,4352]{1,0:T(4,128)} %fused.1) | data formatting | bytes 104448
where the time goes:
time: 35.9 us; the launch traced here: 35.6 us
  Pallas kernels  34.1 us (95%)
  local copies, waits for them, and re-layouts  1.53 us (4%)
    pallas_call x1, Pallas kernels, fast(): pl.pallas_call(functools.partial(fused_kernel, leafs, edges, slots, tiles...  34.1 us
    unnamed x1, local copies, waits for them, and re-layouts  1.53 us

commit v1 on v0

--- a/solution.py
+++ b/solution.py
@@ -11,6 +11,7 @@
 NPT = 544
 LANES = 128
 GROUPS = 4
+CUTS = (33, 46)
 
 reg_square = 0.05
 kernel_scale = 1.0 / (8.0 * math.pi)
@@ -68,17 +69,20 @@
         line = jnp.broadcast_to(part[comp : comp + 1], (16, pos.shape[1])).astype(jnp.bfloat16)
         for r in range(0, rows, 16):
             spread_ref[k * rows + r : k * rows + r + 16, :] = row_ref[r : r + 16, :] * line
-    for comp in range(6):
-        first, count = (comp * 3, 3) if comp < 3 else (6 + comp, 1)
+    for begin, end in ((0, 6), (6, 12)):
         placed = lax.dot_general(
-            spread_ref[first * rows : (first + count) * rows, :], lane_ref[...], NT,
-            preferred_element_type=jnp.float32,
+            spread_ref[begin * rows : end * rows, :], lane_ref[...], NT, preferred_element_type=jnp.float32
         )
-        total = placed[:rows]
-        for part in range(1, count):
-            total = total + placed[part * rows : (part + 1) * rows]
-        for o in range(leafs):
-            send_ref[o, comp] = total[o * win : (o + 1) * win]
+        parts = [placed[r : r + rows] for r in range(0, (end - begin) * rows, rows)]
+        if begin < 9:
+            totals = [parts[r] + parts[r + 1] + parts[r + 2] for r in range(0, min(end, 9) - begin, 3)]
+            totals += parts[9 - begin :]
+        else:
+            totals = parts
+        for k, total in enumerate(totals):
+            comp = begin // 3 + k
+            for o in range(leafs):
+                send_ref[o, comp] = total[o * win : (o + 1) * win]
 
 
 def assemble(starts, recv_ref, tiles_ref):
@@ -134,19 +138,48 @@
     return (sums + pltpu.roll(sums, 5, 0) + pos * sums[6:7]) * kernel_scale
 
 
+def pair_sums(target, sources):
+    weights = jnp.concatenate([weight for weight, _ in sources], axis=1)
+    both = lax.dot_general(target, weights, TN, preferred_element_type=jnp.float32)
+    blocks = []
+    for s in range(len(sources)):
+        first = 2 * LANES * s
+        inverse = lax.rsqrt(both[:, first : first + LANES])
+        along = both[:, first + LANES : first + 2 * LANES] * inverse * (inverse * inverse)
+        blocks.extend(split2(inverse) + split2(along))
+    return lax.dot_general(
+        jnp.concatenate([value for _, value in sources], axis=1), jnp.concatenate(blocks, axis=1), NT,
+        preferred_element_type=jnp.float32,
+    )[:8]
+
+
+def list_steps(begin, end, origin, tiles, lists_ref, tiles_ref, weight_ref, value_ref, target_ref, near_ref):
+    row = lax.broadcasted_iota(jnp.int32, (8, LANES), 0)
+
+    def step(i, carry):
+        j = lax.rem(origin + i, tiles)
+        indices = [tiles + j] + [lists_ref[column, j] for column in range(3)]
+        sums = pair_sums(target_ref[j], [(weight_ref[s], value_ref[s]) for s in indices])
+        pos = jnp.where(row < 3, tiles_ref[1, j], 0.0)
+        near_ref[j] = (sums + pltpu.roll(sums, 5, 0) + pos * sums[6:7]) * kernel_scale
+        return carry
+
+    lax.fori_loop(begin, end, step, 0, unroll=end - begin)
+
+
 def gather(leafs, get_near, row_ref, lane_ref, self_ref, out_ref):
     rows = row_ref.shape[0]
     points = out_ref.shape[1]
     split = []
     for comp in range(3):
         block = jnp.concatenate([get_near(o, comp) for o in range(leafs)], axis=0)
-        split.append(jnp.concatenate([p.astype(jnp.bfloat16) for p in split3(block)], axis=1))
+        split.append(jnp.concatenate(split2(block), axis=1))
     near = jnp.concatenate(split, axis=0)
     for begin in range(0, points, 2 * LANES):
         here = slice(begin, begin + 2 * LANES)
         lane = lane_ref[:, here]
         found = jnp.dot(
-            near, jnp.concatenate([lane, lane, lane], axis=0), preferred_element_type=jnp.float32
+            near, jnp.concatenate([lane, lane], axis=0), preferred_element_type=jnp.float32
         )
         row = row_ref[:, here].astype(jnp.float32)
         for comp in range(3):
@@ -199,14 +232,16 @@
     gather(leafs, lambda o, comp: back_ref[o, comp], row_ref, lane_ref, self_ref, out_ref)
 
 
-def fused_kernel(leafs, edges, slots, tiles, starts, lists_hbm, own_hbm, pos_hbm, den_ref, operator_ref,
-                 out_ref, lists_ref, own_ref, pos_ref, cells_ref, wide_ref, row_ref, lane_ref, spread_ref, send_ref, windows_ref,
+def fused_kernel(leafs, edges, slots, tiles, starts, lists_hbm, own_hbm, pos_hbm, den_hbm, operator_hbm,
+                 out_ref, lists_ref, own_ref, pos_ref, den_ref, operator_ref, cells_ref, wide_ref, row_ref, lane_ref, spread_ref, send_ref, windows_ref,
                  tiles_ref, weight_ref, value_ref, target_ref, near_ref, ret_ref, back_ref,
                  group_ref, partial_ref, parts_ref, whole_ref, self_ref,
                  load_sems, cell_sems, part_sems, point_sems, edge_sems, back_sems):
     loads = [pltpu.make_async_copy(own_hbm, own_ref, load_sems.at[0]),
              pltpu.make_async_copy(pos_hbm, pos_ref, load_sems.at[1]),
-             pltpu.make_async_copy(lists_hbm, lists_ref, load_sems.at[2])]
+             pltpu.make_async_copy(den_hbm, den_ref, load_sems.at[2]),
+             pltpu.make_async_copy(lists_hbm, lists_ref, load_sems.at[3]),
+             pltpu.make_async_copy(operator_hbm, operator_ref, load_sems.at[4])]
     for load in loads:
         load.start()
     leaf, edge = lax.axis_index("leaf"), lax.axis_index("edge")
@@ -266,6 +301,7 @@
     start_forward(leaf, 0)
     for copy in cells:
         copy.wait()
+    loads[4].wait()
     group = group_ref[...].reshape(edges * group_ref.shape[1], group_ref.shape[2])
     partial = lax.dot_general(group, operator_ref[...], NT, preferred_element_type=jnp.float32)
     partial_ref[...] = partial.reshape(partial_ref.shape)
@@ -290,7 +326,7 @@
 
     matrices = (weight_ref, value_ref, target_ref)
     build_layer(tiles, starts, 1, windows_ref.at[1], tiles_ref, *matrices)
-    near_ref[...] = jnp.zeros_like(near_ref)
+    near_ref[tiles:] = jnp.zeros_like(near_ref[tiles:])
     flights = [forward(lax.rem(leaf + leafs - d, leafs), d) for d in range(leafs)]
     for up, down in flights:
         pl.when(has_down)(up.wait_recv)
@@ -302,24 +338,24 @@
     build_layer(tiles, starts, 2, windows_ref.at[2], tiles_ref, *matrices)
 
     win = ret_ref.shape[2]
-
-    unroll = 17 if tiles % 17 == 0 else 1
-    middle = tiles * 2 // 3 // unroll * unroll
-    first = middle * LANES // slots
-    for begin, end, sources in ((0, middle, range(first)), (middle, tiles, range(first, leafs))):
-        near_steps(begin, end, tiles, lists_ref, tiles_ref, *matrices, near_ref, unroll)
-        for s in sources:
+    back = [remote(ret_ref.at[d], back_ref.at[leaf], back_sems, d, leaf=lax.rem(leaf + d, leafs))
+            for d in range(1, leafs)]
+    loads[3].wait()
+    origin = (leaf + 1) * slots // LANES
+    done, sent = 0, 1
+    for end in [cut for cut in CUTS if cut < tiles] + [tiles]:
+        list_steps(done, end, origin, tiles, lists_ref, tiles_ref, *matrices, near_ref)
+        done = end
+        while sent < leafs and (sent * slots + LANES - 1) // LANES + 1 <= done:
+            to = lax.rem(leaf + sent, leafs)
+            first = to * slots // LANES
             for comp in range(3):
-                ret_ref[s, comp] = near_ref[starts[s] : starts[s] + win, comp, :]
-
-            @pl.when(leaf != s)
-            def _(s=s):
-                give = pltpu.make_async_remote_copy(
-                    src_ref=ret_ref.at[s], dst_ref=back_ref.at[leaf], send_sem=back_sems.at[0, s],
-                    recv_sem=back_sems.at[1, leaf], device_id={"leaf": s})
-                give.start()
-
-    back_ref[leaf] = ret_ref[leaf]
+                ret_ref[sent, comp] = near_ref[pl.ds(first, win), comp, :]
+            back[sent - 1].start()
+            sent += 1
+    first = leaf * slots // LANES
+    for comp in range(3):
+        back_ref[leaf, comp] = near_ref[pl.ds(first, win), comp, :]
     for copy in parts:
         copy.wait()
     share = parts_ref.shape[2]
@@ -328,13 +364,8 @@
     for c in range(count):
         for k in range(3):
             self_ref[k : k + 1, c * NPT : (c + 1) * NPT] = whole_ref[c : c + 1, k * NPT : (k + 1) * NPT]
-    for s in range(leafs):
-        @pl.when(leaf != s)
-        def _(s=s):
-            take = pltpu.make_async_remote_copy(
-                src_ref=ret_ref.at[s], dst_ref=back_ref.at[s], send_sem=back_sems.at[0, s],
-                recv_sem=back_sems.at[1, s], device_id={"leaf": s})
-            take.wait()
+    for copy in back:
+        copy.wait()
     gather(leafs, lambda o, comp: back_ref[o, comp], row_ref, lane_ref, self_ref, out_ref)
 
 
@@ -374,12 +405,14 @@
         return pl.pallas_call(
             functools.partial(fused_kernel, leafs, edges, slots, tiles, starts),
             out_shape=shape((3, points), f32),
-            in_specs=[pl.BlockSpec(memory_space=pltpu.HBM)] * 3 + [VM] * 2,
+            in_specs=[pl.BlockSpec(memory_space=pltpu.HBM)] * 5,
             out_specs=VM,
             scratch_shapes=[
                 pltpu.SMEM((3, tiles), jnp.int32),
                 pltpu.VMEM((1, points), jnp.int32),
                 pltpu.VMEM((3, points), f32),
+                pltpu.VMEM((3, points), bf16),
+                pltpu.VMEM(self_operator.shape, bf16),
                 pltpu.VMEM((group, 3 * NPT), bf16),
                 pltpu.VMEM((group, 3 * NPT), f32),
                 pltpu.VMEM((rows, points), bf16),
@@ -395,7 +428,7 @@
                 pltpu.VMEM((edges, cell_count, self_operator.shape[0]), f32),
                 pltpu.VMEM((cell_count, 3 * NPT), f32),
                 pltpu.VMEM((3, points), f32),
-                sems((3,)), sems((2, edges)), sems((2, edges)), sems((2, leafs)), sems((2, 2, leafs)),
+                sems((5,)), sems((2, edges)), sems((2, edges)), sems((2, leafs)), sems((2, 2, leafs)),
                 sems((2, leafs)),
             ],
             compiler_params=pltpu.CompilerParams(

time: 35.9 us -> 32.3 us (0.90)
  Pallas kernels: 34.1 us -> 30.6 us
    pallas_call x1, Pallas kernels: 34.1 us -> 30.6 us  [fast(): pl.pallas_call(functools.partial(fused_kernel, leafs, edges, slots, tiles...]
where the time goes in v1:
time: 32.3 us; the launch traced here: 32.1 us
  Pallas kernels  30.6 us (95%)
  local copies, waits for them, and re-layouts  1.53 us (5%)
    pallas_call x1, Pallas kernels, fast(): pl.pallas_call(functools.partial(fused_kernel, leafs, edges, slots, tiles...  30.6 us
    unnamed x1, local copies, waits for them, and re-layouts  1.53 us

profile of v1, /device:TPU:1, one launch (start us, length us, event | category | flops | bytes accessed | tf_op | source)
XLA Modules:
  0.0 32.1 jit_solution(11448548434645544925)
XLA Ops:
  0.0 30.6 %fused.1 = f32[3,4352]{1,0:T(4,128)} custom-call(s32[3,51]{1,0:T(4,128)} %bitcast.3, s32[1,4352]{1,0:T(1,128)} %bitcast.2, f32[3,4352]{1,0:T(4,128)} %pos_hbm.1, bf16[3,4352]{1,0:T(4,128)(2,1)} %den_hbm.1, bf16[408,1632]{1,0:T(8,128)(2,1)} %operator_hbm.1), custom_call_target="tpu_custom_call" | custom-call | tf_op jit(solution)/shard_map/fused/pallas_call | solution.py:405
  30.6 1.5 %copy.7 = f32[3,4352]{1,0:T(4,128)} copy(f32[3,4352]{1,0:T(4,128)} %fused.1) | data formatting | bytes 104448

commit v2 on v1

--- a/solution.py
+++ b/solution.py
@@ -85,6 +85,40 @@
                 send_ref[o, comp] = total[o * win : (o + 1) * win]
 
 
+def scatter_halves(leafs, pos_ref, den_ref, row_ref, lane_ref, spread_ref, send_ref):
+    rows = row_ref.shape[0]
+    win = rows // leafs
+    pos = pos_ref[...]
+    den = den_ref[...].astype(jnp.float32)
+    high = pos.astype(jnp.bfloat16).astype(jnp.float32)
+    parts = (high, pos - high)
+    for k in range(9):
+        part, comp = (parts[k % 2], k // 2) if k < 6 else (den, k - 6)
+        line = jnp.broadcast_to(part[comp : comp + 1], (16, pos.shape[1])).astype(jnp.bfloat16)
+        for r in range(0, rows, 16):
+            spread_ref[k * rows + r : k * rows + r + 16, :] = row_ref[r : r + 16, :] * line
+    placed = []
+    for begin, end in ((0, 5), (5, 9)):
+        found = lax.dot_general(
+            spread_ref[begin * rows : end * rows, :], lane_ref[...], NT, preferred_element_type=jnp.float32
+        )
+        placed += [found[k * rows : (k + 1) * rows] for k in range(end - begin)]
+    empty = jnp.zeros((send_ref.shape[1] - 9 * win, LANES), jnp.float32)
+    for o in range(leafs):
+        here = [part[o * win : (o + 1) * win] for part in placed] + [empty]
+        send_ref[o] = jnp.concatenate(here, axis=0).astype(jnp.bfloat16)
+
+
+def assemble_halves(starts, win, recv_ref, tiles_ref):
+    tiles_ref[...] = jnp.zeros_like(tiles_ref)
+    for l, start in enumerate(starts):
+        window = recv_ref[l].astype(jnp.float32)
+        parts = [window[k * win : (k + 1) * win] for k in range(9)]
+        comps = [parts[0] + parts[1], parts[2] + parts[3], parts[4] + parts[5]] + parts[6:]
+        for comp in range(6):
+            tiles_ref[start : start + win, comp, :] += comps[comp]
+
+
 def assemble(starts, recv_ref, tiles_ref):
     tiles_ref[...] = jnp.zeros_like(tiles_ref)
     win = recv_ref.shape[2]
@@ -195,8 +229,11 @@
     scatter(leafs, pos_ref, den_ref, row_ref, lane_ref, spread_ref, send_ref)
 
 
-def build_layer(tiles, starts, layer, recv, tiles_ref, weight_ref, value_ref, target_ref):
-    assemble(starts, recv, tiles_ref.at[layer])
+def build_layer(tiles, starts, layer, recv, tiles_ref, weight_ref, value_ref, target_ref, win=None):
+    if win is None:
+        assemble(starts, recv, tiles_ref.at[layer])
+    else:
+        assemble_halves(starts, win, recv, tiles_ref.at[layer])
 
     def build(j, carry):
         index = layer * tiles + j
@@ -244,6 +281,7 @@
              pltpu.make_async_copy(operator_hbm, operator_ref, load_sems.at[4])]
     for load in loads:
         load.start()
+    win = ret_ref.shape[2]
     leaf, edge = lax.axis_index("leaf"), lax.axis_index("edge")
     barrier = pltpu.get_barrier_semaphore()
     for d in range(1, leafs):
@@ -261,7 +299,7 @@
     onehots(leafs, lax.rem(leaf * slots, LANES), own_ref, row_ref, lane_ref)
     loads[1].wait()
     loads[2].wait()
-    scatter(leafs, pos_ref, den_ref, row_ref, lane_ref, spread_ref, send_ref)
+    scatter_halves(leafs, pos_ref, den_ref, row_ref, lane_ref, spread_ref, send_ref)
     pl.semaphore_wait(barrier, leafs + edges - 2)
 
     points = []
@@ -325,19 +363,18 @@
         windows_ref[2] = jnp.zeros_like(windows_ref[2])
 
     matrices = (weight_ref, value_ref, target_ref)
-    build_layer(tiles, starts, 1, windows_ref.at[1], tiles_ref, *matrices)
+    build_layer(tiles, starts, 1, windows_ref.at[1], tiles_ref, *matrices, win=win)
     near_ref[tiles:] = jnp.zeros_like(near_ref[tiles:])
     flights = [forward(lax.rem(leaf + leafs - d, leafs), d) for d in range(leafs)]
     for up, down in flights:
         pl.when(has_down)(up.wait_recv)
-    build_layer(tiles, starts, 0, windows_ref.at[0], tiles_ref, *matrices)
+    build_layer(tiles, starts, 0, windows_ref.at[0], tiles_ref, *matrices, win=win)
     for up, down in flights:
         pl.when(has_up)(down.wait_recv)
         pl.when(has_up)(up.wait_send)
         pl.when(has_down)(down.wait_send)
-    build_layer(tiles, starts, 2, windows_ref.at[2], tiles_ref, *matrices)
-
-    win = ret_ref.shape[2]
+    build_layer(tiles, starts, 2, windows_ref.at[2], tiles_ref, *matrices, win=win)
+
     back = [remote(ret_ref.at[d], back_ref.at[leaf], back_sems, d, leaf=lax.rem(leaf + d, leafs))
             for d in range(1, leafs)]
     loads[3].wait()
@@ -401,6 +438,7 @@
     ]
     if leafs <= 8:
         group = -(-cell_count // 16) * 16
+        sent = -(-9 * win // 16) * 16
         sems = pltpu.SemaphoreType.DMA
         return pl.pallas_call(
             functools.partial(fused_kernel, leafs, edges, slots, tiles, starts),
@@ -417,9 +455,9 @@
                 pltpu.VMEM((group, 3 * NPT), f32),
                 pltpu.VMEM((rows, points), bf16),
                 pltpu.VMEM((LANES, points), bf16),
-                pltpu.VMEM((12 * rows, points), bf16),
-                pltpu.VMEM((leafs, 6, win, LANES), f32),
-                pltpu.VMEM((3, leafs, 6, win, LANES), f32),
+                pltpu.VMEM((9 * rows, points), bf16),
+                pltpu.VMEM((leafs, sent, LANES), bf16),
+                pltpu.VMEM((3, leafs, sent, LANES), bf16),
                 *matrices,
                 pltpu.VMEM((leafs, 3, win, LANES), f32),
                 pltpu.VMEM((leafs, 3, win, LANES), f32),

time: 32.3 us -> 31.5 us (0.975)
  Pallas kernels: 30.6 us -> 29.8 us
    pallas_call x1, Pallas kernels: 30.6 us -> 29.8 us  [fast(): pl.pallas_call(functools.partial(fused_kernel, leafs, edges, slots, tiles...]
where the time goes in v2:
time: 31.5 us; the launch traced here: 31.3 us
  Pallas kernels  29.8 us (95%)
  local copies, waits for them, and re-layouts  1.53 us (5%)
    pallas_call x1, Pallas kernels, fast(): pl.pallas_call(functools.partial(fused_kernel, leafs, edges, slots, tiles...  29.8 us
    unnamed x1, local copies, waits for them, and re-layouts  1.53 us

profile of v2, /device:TPU:1, one launch (start us, length us, event | category | flops | bytes accessed | tf_op | source)
XLA Modules:
  0.0 31.3 jit_solution(10023220553201598492)
XLA Ops:
  0.0 29.8 %fused.1 = f32[3,4352]{1,0:T(4,128)} custom-call(s32[3,51]{1,0:T(4,128)} %bitcast.3, s32[1,4352]{1,0:T(1,128)} %bitcast.2, f32[3,4352]{1,0:T(4,128)} %pos_hbm.1, bf16[3,4352]{1,0:T(4,128)(2,1)} %den_hbm.1, bf16[408,1632]{1,0:T(8,128)(2,1)} %operator_hbm.1), custom_call_target="tpu_custom_call" | custom-call | tf_op jit(solution)/shard_map/fused/pallas_call | solution.py:443
  29.8 1.5 %copy.7 = f32[3,4352]{1,0:T(4,128)} copy(f32[3,4352]{1,0:T(4,128)} %fused.1) | data formatting | bytes 104448

commit v3 on v2

--- a/solution.py
+++ b/solution.py
@@ -109,14 +109,18 @@
         send_ref[o] = jnp.concatenate(here, axis=0).astype(jnp.bfloat16)
 
 
+def add_window(start, win, window, tiles_ref):
+    window = window.astype(jnp.float32)
+    parts = [window[k * win : (k + 1) * win] for k in range(9)]
+    comps = [parts[0] + parts[1], parts[2] + parts[3], parts[4] + parts[5]] + parts[6:]
+    for comp in range(6):
+        tiles_ref[pl.ds(start, win), comp, :] += comps[comp]
+
+
 def assemble_halves(starts, win, recv_ref, tiles_ref):
     tiles_ref[...] = jnp.zeros_like(tiles_ref)
     for l, start in enumerate(starts):
-        window = recv_ref[l].astype(jnp.float32)
-        parts = [window[k * win : (k + 1) * win] for k in range(9)]
-        comps = [parts[0] + parts[1], parts[2] + parts[3], parts[4] + parts[5]] + parts[6:]
-        for comp in range(6):
-            tiles_ref[start : start + win, comp, :] += comps[comp]
+        add_window(start, win, recv_ref[l], tiles_ref)
 
 
 def assemble(starts, recv_ref, tiles_ref):
@@ -232,7 +236,7 @@
 def build_layer(tiles, starts, layer, recv, tiles_ref, weight_ref, value_ref, target_ref, win=None):
     if win is None:
         assemble(starts, recv, tiles_ref.at[layer])
-    else:
+    elif layer != 1:
         assemble_halves(starts, win, recv, tiles_ref.at[layer])
 
     def build(j, carry):
@@ -241,7 +245,7 @@
                  target_ref.at[j] if layer == 1 else None)
         return carry
 
-    lax.fori_loop(0, tiles, build, 0, unroll=3)
+    lax.fori_loop(0, tiles, build, 0, unroll=17)
 
 
 def near_steps(begin, end, tiles, lists_ref, tiles_ref, weight_ref, value_ref, target_ref, near_ref, unroll):
@@ -337,6 +341,8 @@
         pl.when(has_down)(down.start)
 
     start_forward(leaf, 0)
+    tiles_ref[1] = jnp.zeros_like(tiles_ref[1])
+    add_window(leaf * slots // LANES, win, send_ref[leaf], tiles_ref.at[1])
     for copy in cells:
         copy.wait()
     loads[4].wait()
@@ -352,7 +358,9 @@
 
     for d in range(1, leafs):
         points[d - 1].wait()
-        start_forward(lax.rem(leaf + leafs - d, leafs), d)
+        source = lax.rem(leaf + leafs - d, leafs)
+        start_forward(source, d)
+        add_window(source * slots // LANES, win, windows_ref[1, source], tiles_ref.at[1])
 
     @pl.when(edge == 0)
     def _():

time: 31.5 us -> 31.4 us (level)
  no operation moved by 1% of the time
where the time goes in v3:
time: 31.4 us; the launch traced here: 31.2 us
  Pallas kernels  29.6 us (94%)
  local copies, waits for them, and re-layouts  1.53 us (5%)
    pallas_call x1, Pallas kernels, fast(): pl.pallas_call(functools.partial(fused_kernel, leafs, edges, slots, tiles...  29.6 us
    unnamed x1, local copies, waits for them, and re-layouts  1.53 us

profile of v3, /device:TPU:1, one launch (start us, length us, event | category | flops | bytes accessed | tf_op | source)
XLA Modules:
  0.0 31.2 jit_solution(10021033090801712685)
XLA Ops:
  0.0 29.6 %fused.1 = f32[3,4352]{1,0:T(4,128)} custom-call(s32[3,51]{1,0:T(4,128)} %bitcast.3, s32[1,4352]{1,0:T(1,128)} %bitcast.2, f32[3,4352]{1,0:T(4,128)} %pos_hbm.1, bf16[3,4352]{1,0:T(4,128)(2,1)} %den_hbm.1, bf16[408,1632]{1,0:T(8,128)(2,1)} %operator_hbm.1), custom_call_target="tpu_custom_call" | custom-call | tf_op jit(solution)/shard_map/fused/pallas_call | solution.py:451
  29.7 1.5 %copy.7 = f32[3,4352]{1,0:T(4,128)} copy(f32[3,4352]{1,0:T(4,128)} %fused.1) | data formatting | bytes 104448

commit v4 on v3

--- a/solution.py
+++ b/solution.py
@@ -177,8 +177,11 @@
 
 
 def pair_sums(target, sources):
-    weights = jnp.concatenate([weight for weight, _ in sources], axis=1)
-    both = lax.dot_general(target, weights, TN, preferred_element_type=jnp.float32)
+    halves = []
+    for s in range(0, len(sources), 2):
+        weights = jnp.concatenate([weight for weight, _ in sources[s : s + 2]], axis=1)
+        halves.append(lax.dot_general(target, weights, TN, preferred_element_type=jnp.float32))
+    both = jnp.concatenate(halves, axis=1)
     blocks = []
     for s in range(len(sources)):
         first = 2 * LANES * s

time: 31.4 us -> 31.4 us (level)
  no operation moved by 1% of the time
where the time goes in v4:
time: 31.4 us; the launch traced here: 31.2 us
  Pallas kernels  29.6 us (94%)
  local copies, waits for them, and re-layouts  1.53 us (5%)
    pallas_call x1, Pallas kernels, fast(): pl.pallas_call(functools.partial(fused_kernel, leafs, edges, slots, tiles...  29.6 us
    unnamed x1, local copies, waits for them, and re-layouts  1.53 us

profile of v4, /device:TPU:1, one launch (start us, length us, event | category | flops | bytes accessed | tf_op | source)
XLA Modules:
  0.0 31.2 jit_solution(10021033090801712685)
XLA Ops:
  0.0 29.6 %fused.1 = f32[3,4352]{1,0:T(4,128)} custom-call(s32[3,51]{1,0:T(4,128)} %bitcast.3, s32[1,4352]{1,0:T(1,128)} %bitcast.2, f32[3,4352]{1,0:T(4,128)} %pos_hbm.1, bf16[3,4352]{1,0:T(4,128)(2,1)} %den_hbm.1, bf16[408,1632]{1,0:T(8,128)(2,1)} %operator_hbm.1), custom_call_target="tpu_custom_call" | custom-call | tf_op jit(solution)/shard_map/fused/pallas_call | solution.py:454
  29.7 1.5 %copy.7 = f32[3,4352]{1,0:T(4,128)} copy(f32[3,4352]{1,0:T(4,128)} %fused.1) | data formatting | bytes 104448
